TPU v7x, 256 devices: a whole 4x4x8 slice. The times are simulated.
256 devices in a mesh: blk: 32 (over y_hi, z, core), uly: 8 (over x, y_lo).
Axes of the slice: x: 4, y: 4 (y_hi: 2, y_lo: 2; y = y_hi * 2 + y_lo), z: 8, core: 2. Of those that a mesh axis runs over, the one named last changes fastest.
Arguments:
- query_rows: bfloat16 [65536, 1024], P(('blk', 'uly')), may hold values from -6 to 6
- key_rows: bfloat16 [65536, 128], P('blk'), may hold values from -6 to 6
- value_rows: bfloat16 [65536, 128], P('blk'), may hold values from -6 to 6
- forward_output: bfloat16 [65536, 1024], P('blk', 'uly'), may hold values from -6 to 6
- grad_output: bfloat16 [65536, 1024], P(('blk', 'uly')), may hold values from -48 to 48
- log_normalizer: float32 [8, 65536], P('uly', 'blk'), may hold values from 1 to 9
- block_order: int32 [64], replicated, may hold values from 0 to 63, as said below
- block_table: int32 [64, 64], replicated, may hold values 0 or 1
Outputs:
- grad_query: bfloat16 [65536, 1024], P(('blk', 'uly'))
- grad_key: bfloat16 [65536, 128], P(('blk', 'uly'))
- grad_value: bfloat16 [65536, 128], P(('blk', 'uly'))
Inputs may be any that keep to these rules, and one draw needn't show every extreme that they name: `block_order`: stored blocks 2 i and 2 i + 1 hold sequence blocks b and 63 - b for some b; each of 0 to 63 appears once.
All inputs are finite; a program needn't handle non-finite values.
Results may differ from a plain program's by a relative error of at most 0.0065.
Values may be sent and summed in bfloat16 or wider, within the bound.
A program may use at most 128 MiB of HBM per device.

v0:
```python
import math

import jax
import jax.numpy as jnp
from jax import lax
from jax.sharding import PartitionSpec as P


def shifted(value, axis, steps):
    count = lax.axis_size(axis)
    pairs = [(source, (source + steps) % count) for source in range(count)]
    return lax.ppermute(value, axis, pairs)


def pair_mask(q_seq, k_seq, block_table, tile_rows):
    causal_tri = lax.broadcasted_iota(jnp.int32, (tile_rows, tile_rows), 0) >= lax.broadcasted_iota(
        jnp.int32, (tile_rows, tile_rows), 1
    )
    earlier = (k_seq < q_seq) & (block_table[q_seq, k_seq] == 1)
    return jnp.where(k_seq == q_seq, causal_tri, jnp.broadcast_to(earlier, (tile_rows, tile_rows)))


def tile_gradients(q_tile, g_tile, norm_tile, delta_tile, k_tile, v_tile, allowed, attn_scale):
    scores = (
        jnp.einsum("qhd,kd->hqk", q_tile, k_tile, preferred_element_type=jnp.float32) * attn_scale
    )
    probs = jnp.where(allowed[None], jnp.exp(scores - norm_tile[:, :, None]), 0.0)
    grad_v = jnp.einsum(
        "hqk,qhd->kd", probs.astype(jnp.bfloat16), g_tile, preferred_element_type=jnp.float32
    )
    grad_probs = jnp.einsum("qhd,kd->hqk", g_tile, v_tile, preferred_element_type=jnp.float32)
    grad_scores = (probs * (grad_probs - delta_tile[:, :, None])).astype(jnp.bfloat16)
    grad_q = (
        jnp.einsum("hqk,kd->qhd", grad_scores, k_tile, preferred_element_type=jnp.float32)
        * attn_scale
    )
    grad_k = (
        jnp.einsum("hqk,qhd->kd", grad_scores, q_tile, preferred_element_type=jnp.float32)
        * attn_scale
    )
    return (grad_q, grad_k, grad_v)


def block_gradients(
    queries,
    out_grads,
    norm_rows,
    delta_rows,
    q_seqs,
    key_tiles,
    value_tiles,
    k_seqs,
    block_table,
    attn_scale,
):
    tile_rows = queries.shape[0] // 2
    width = key_tiles.shape[1]
    query_parts = []
    key_parts = [jnp.zeros((tile_rows, width), jnp.float32) for _ in range(2)]
    value_parts = [jnp.zeros((tile_rows, width), jnp.float32) for _ in range(2)]
    for query_half in range(2):
        low = query_half * tile_rows
        row_part = jnp.zeros((tile_rows,) + queries.shape[1:], jnp.float32)
        for key_half in range(2):
            first = key_half * tile_rows
            allowed = pair_mask(q_seqs[query_half], k_seqs[key_half], block_table, tile_rows)
            q_tile = queries[low : low + tile_rows]
            g_tile = out_grads[low : low + tile_rows]
            norm_tile = norm_rows[:, low : low + tile_rows]
            delta_tile = delta_rows[:, low : low + tile_rows]
            k_tile = key_tiles[first : first + tile_rows]
            v_tile = value_tiles[first : first + tile_rows]
            outcome = tile_gradients(
                q_tile, g_tile, norm_tile, delta_tile, k_tile, v_tile, allowed, attn_scale
            )
            row_part = row_part + outcome[0]
            key_parts[key_half] = key_parts[key_half] + outcome[1]
            value_parts[key_half] = value_parts[key_half] + outcome[2]
        query_parts.append(row_part)
    return (
        jnp.concatenate(query_parts, axis=0),
        jnp.concatenate(key_parts, axis=0),
        jnp.concatenate(value_parts, axis=0),
    )


def body(
    query_rows,
    key_rows,
    value_rows,
    forward_output,
    grad_output,
    log_normalizer,
    block_order,
    block_table,
):
    head_dim = key_rows.shape[1]
    attn_scale = 1.0 / math.sqrt(head_dim)
    query_heads, cotangent_heads = (
        lax.all_to_all(query_rows, "uly", split_axis=1, concat_axis=0, tiled=True),
        lax.all_to_all(grad_output, "uly", split_axis=1, concat_axis=0, tiled=True),
    )
    total_rows = query_heads.shape[0]
    local_heads = query_heads.shape[1] // head_dim
    queries = query_heads.reshape(total_rows, local_heads, head_dim)
    out_grads = cotangent_heads.reshape(total_rows, local_heads, head_dim)
    outputs = forward_output.reshape(total_rows, local_heads, head_dim)
    delta_rows = jnp.einsum("qhd,qhd->hq", out_grads, outputs, preferred_element_type=jnp.float32)
    block_count = lax.axis_size("blk")
    group_index = lax.axis_index("blk")

    def stored_blocks(owner_index):
        return (block_order[2 * owner_index], block_order[2 * owner_index + 1])

    home_seqs = stored_blocks(group_index)
    query_sum, key_sum, value_sum = block_gradients(
        queries,
        out_grads,
        log_normalizer,
        delta_rows,
        home_seqs,
        key_rows,
        value_rows,
        home_seqs,
        block_table,
        attn_scale,
    )
    moving_keys, moving_values = (key_rows, value_rows)
    moving_keys, moving_values = shifted((moving_keys, moving_values), "blk", 1)
    owner_index = (group_index - 1) % block_count
    grad_q, grad_k, grad_v = block_gradients(
        queries,
        out_grads,
        log_normalizer,
        delta_rows,
        home_seqs,
        moving_keys,
        moving_values,
        stored_blocks(owner_index),
        block_table,
        attn_scale,
    )
    query_sum = query_sum + grad_q
    back_key, back_value = shifted((grad_k, grad_v), "blk", -1)
    key_sum = key_sum + back_key
    value_sum = value_sum + back_value
    key_part, value_part = (
        lax.psum_scatter(key_sum, "uly", scatter_dimension=0, tiled=True),
        lax.psum_scatter(value_sum, "uly", scatter_dimension=0, tiled=True),
    )
    query_half_rows = query_sum.reshape(total_rows, local_heads * head_dim).astype(jnp.bfloat16)
    grad_query = lax.all_to_all(query_half_rows, "uly", split_axis=0, concat_axis=1, tiled=True)
    return (grad_query, key_part.astype(jnp.bfloat16), value_part.astype(jnp.bfloat16))


def solution(mesh):
    in_specs = (
        P(("blk", "uly"), None),
        P("blk", None),
        P("blk", None),
        P("blk", "uly"),
        P(("blk", "uly"), None),
        P("uly", "blk"),
        P(),
        P(),
    )
    out_specs = (P(("blk", "uly"), None), P(("blk", "uly"), None), P(("blk", "uly"), None))
    return jax.shard_map(body, mesh=mesh, in_specs=in_specs, out_specs=out_specs, check_vma=False)
```

profile of v0, /device:TPU:32, one launch (start us, length us, event | category | flops | bytes accessed | tf_op | source)
XLA Modules:
  0.0 229.7 jit_solution(6731134996444053685)
XLA Ops:
  7.2 2.0 copy.15
  9.2 5.4 %all-to-all-start.1 = ((bf16[256,8,128]{0,2,1:T(8,128)(2,1)}), bf16[256,8,128]{0,2,1:T(8,128)(2,1)S(1)}, u32[]{:S(2)}, u32[]{:S(2)}) async-start(bf16[256,8,128]{0,2,1:T(8,128)(2,1)} %bitcast.6), calls=%async_computation.1 | async-start | bytes 1048576 | tf_op jit(solution)/shard_map/all_to_all | solution.py:101
  14.7 2.0 collective-permute-start
  46.4 2.0 copy.13
  48.5 5.7 %all-to-all-start = ((bf16[256,8,128]{0,2,1:T(8,128)(2,1)}), bf16[256,8,128]{0,2,1:T(8,128)(2,1)S(1)}, u32[]{:S(2)}, u32[]{:S(2)}) async-start(bf16[256,8,128]{0,2,1:T(8,128)(2,1)} %bitcast), calls=%async_computation | async-start | bytes 1048576 | tf_op jit(solution)/shard_map/all_to_all | solution.py:100
  55.0 8.8 %all-to-all-done = bf16[256,8,128]{0,2,1:T(8,128)(2,1)S(1)} async-done(((bf16[256,8,128]{0,2,1:T(8,128)(2,1)}), bf16[256,8,128]{0,2,1:T(8,128)(2,1)S(1)}, u32[]{:S(2)}, u32[]{:S(2)}) %all-to-all-start) | async-done | bytes 524320 | tf_op jit(solution)/shard_map/all_to_all | solution.py:100
  70.3 2.7 %fusion.187 = f32[1024,1024]{1,0:T(8,128)} fusion(bf16[1024,128]{1,0:T(8,128)(2,1)S(1)} %bitcast.427, bf16[2048,128]{1,0:T(8,128)(2,1)S(1)} %copy-done.8), kind=kOutput, calls=%fused_computation.179 | convolution fusion | flops 268435456 | bytes 4718592 | tf_op jit(solution)/shard_map/qhd,kd->hqk/dot_general | solution.py:25
  73.1 2.7 %fusion.184 = f32[1024,1024]{1,0:T(8,128)} fusion(bf16[1024,128]{1,0:T(8,128)(2,1)S(1)} %bitcast.433, bf16[2048,128]{1,0:T(8,128)(2,1)S(1)} %copy-done.8), kind=kOutput, calls=%fused_computation.176 | convolution fusion | flops 268435456 | bytes 4718592 | tf_op jit(solution)/shard_map/qhd,kd->hqk/dot_general | solution.py:25
  75.9 2.7 %fusion.190 = f32[1024,1024]{1,0:T(8,128)} fusion(bf16[1024,128]{1,0:T(8,128)(2,1)S(1)} %bitcast.434, bf16[2048,128]{1,0:T(8,128)(2,1)S(1)} %copy-done.8), kind=kOutput, calls=%fused_computation.182 | convolution fusion | flops 268435456 | bytes 4718592 | tf_op jit(solution)/shard_map/qhd,kd->hqk/dot_general | solution.py:25
  79.4 3.5 %fusion.10 = bf16[1,1024,1024]{1,2,0:T(8,128)(2,1)S(1)} fusion(f32[1024,1024]{1,0:T(8,128)} %fusion.187, bf16[1024,128]{1,0:T(8,128)(2,1)S(1)} %bitcast.447, f32[1024]{0:T(1024)S(1)} %bitcast.483, f32[1024]{0:T(1024)S(1)} %bitcast.464, pred[]{:T(512)S(6)} %and.25, pred[]{:T(512)S(6)} %eq.59, bf16[2048,128]{1,0:T(8,128)(2,1)} %param.10), kind=kOutput, calls=%fused_computation.31 | convolution fusion | flops 276824064 | bytes 6823938 | tf_op jit(solution)/shard_map/qhd,kd->hqk/dot_general | solution.py:31
  83.7 1.6 fusion.119
  94.2 2.4 %fusion.2 = bf16[1,1024,1024]{1,2,0:T(8,128)(2,1)S(1)} fusion(f32[1024,1024]{1,0:T(8,128)S(1)} %fusion.175, bf16[1024,128]{1,0:T(8,128)(2,1)S(1)} %bitcast.448, f32[1024]{0:T(1024)S(1)} %bitcast.484, f32[1024]{0:T(1024)S(1)} %bitcast.465, pred[]{:T(512)S(6)} %and.29, pred[]{:T(512)S(6)} %eq.68, bf16[2048,128]{1,0:T(8,128)(2,1)} %collective-permute-done.1), kind=kOutput, calls=%fused_computation.7 | convolution fusion | flops 276824064 | bytes 6823938 | tf_op jit(solution)/shard_map/qhd,kd->hqk/dot_general | solution.py:31
  98.2 2.3 %fusion = bf16[1,1024,1024]{1,2,0:T(8,128)(2,1)S(1)} fusion(f32[1024,1024]{1,0:T(8,128)S(1)} %fusion.169, bf16[1024,128]{1,0:T(8,128)(2,1)S(1)} %bitcast.449, f32[1024]{0:T(1024)S(1)} %bitcast.485, f32[1024]{0:T(1024)S(1)} %bitcast.466, pred[]{:T(512)S(6)} %and.30, pred[]{:T(512)S(6)} %eq.71, bf16[2048,128]{1,0:T(8,128)(2,1)} %collective-permute-done.1), kind=kOutput, calls=%fused_computation.1 | convolution fusion | flops 276824064 | bytes 6823938 | tf_op jit(solution)/shard_map/qhd,kd->hqk/dot_general | solution.py:31
  101.9 2.3 fusion.4
  105.6 2.2 fusion.6
  109.9 1.7 fusion.78
  111.6 1.8 fusion.146
  113.4 8.0 %collective-permute-done.2 = f32[2048,128]{1,0:T(8,128)S(1)} collective-permute-done((f32[2048,128]{1,0:T(8,128)S(1)}, f32[2048,128]{1,0:T(8,128)S(1)}, u32[]{:S(2)}, u32[]{:S(2)}) %collective-permute-start.2) | collective-permute-done | bytes 1048608 | tf_op jit(solution)/shard_map/ppermute | solution.py:12
  122.6 3.4 %fusion.149 = f32[1024,128]{1,0:T(8,128)S(1)} fusion(f32[1024,128]{1,0:T(8,128)} %fusion.78, bf16[1024,128]{1,0:T(8,128)(2,1)S(1)} %bitcast.451, f32[1024,1024]{1,0:T(8,128)} %copy-done.16, f32[1024]{0:T(1024)S(1)} %bitcast.468, pred[]{:T(512)S(6)} %and.29, pred[]{:T(512)S(6)} %eq.68), kind=kOutput, calls=%fused_computation.140 | convolution fusion | flops 274857984 | bytes 5509122 | tf_op jit(solution)/shard_map/hqk,qhd->kd/dot_general | solution.py:28
  126.1 2.0 collective-permute-start.3
  132.9 7.5 %collective-permute-done.3 = f32[2048,128]{1,0:T(8,128)S(1)} collective-permute-done((f32[2048,128]{1,0:T(8,128)S(1)}, f32[2048,128]{1,0:T(8,128)S(1)}, u32[]{:S(2)}, u32[]{:S(2)}) %collective-permute-start.3) | collective-permute-done | bytes 1048608 | tf_op jit(solution)/shard_map/ppermute | solution.py:12
  146.2 14.9 %all_to_all.48 = bf16[8,256,128]{2,1,0:T(8,128)(2,1)S(1)} all-to-all(bf16[8,256,128]{2,1,0:T(8,128)(2,1)S(1)} %bitcast.443), channel_id=1, replica_groups=mesh['blk'=32,'uly'=8] {'uly'}, dimensions={0} | all-to-all | bytes 1048576 | tf_op jit(solution)/shard_map/all_to_all | solution.py:152
  161.9 8.1 %reduce-scatter.3.cloned.1.call-done = f32[256,128]{1,0:T(8,128)} async-done(((f32[2048,128]{1,0:T(8,128)}), f32[256,128]{1,0:T(8,128)}) %reduce-scatter.3.cloned.1.call-update) | async-done | bytes 131088 | tf_op jit(solution)/shard_map/reduce_scatter | solution.py:148
  171.6 49.6 %reduce-scatter.5.cloned.1.call-done = f32[256,128]{1,0:T(8,128)} async-done(((f32[2048,128]{1,0:T(8,128)}), f32[256,128]{1,0:T(8,128)}) %reduce-scatter.5.cloned.1.call-update) | async-done | bytes 131088 | tf_op jit(solution)/shard_map/reduce_scatter | solution.py:149
  (117 shorter events, 42.7 us)
Async XLA Ops:
  7.2 47.5 %copy-start.25 = (f32[1,2048]{1,0:T(1,128)S(1)}, f32[1,2048]{1,0:T(1,128)}, u32[]{:S(2)}) copy-start(f32[1,2048]{1,0:T(1,128)} %param.13) | copy-start | bytes 24580
  9.2 56.5 %copy-start.8 = (bf16[2048,128]{1,0:T(8,128)(2,1)S(1)}, bf16[2048,128]{1,0:T(8,128)(2,1)}, u32[]{:S(2)}) copy-start(bf16[2048,128]{1,0:T(8,128)(2,1)} %param.9) | copy-start | bytes 1572868
  9.2 39.3 %all-to-all-start.1 = ((bf16[256,8,128]{0,2,1:T(8,128)(2,1)}), bf16[256,8,128]{0,2,1:T(8,128)(2,1)S(1)}, u32[]{:S(2)}, u32[]{:S(2)}) async-start(bf16[256,8,128]{0,2,1:T(8,128)(2,1)} %bitcast.6), calls=%async_computation.1 | async-start | bytes 1048576 | tf_op jit(solution)/shard_map/all_to_all | solution.py:101
  14.7 79.6 %collective-permute-start.1 = (bf16[2048,128]{1,0:T(8,128)(2,1)}, bf16[2048,128]{1,0:T(8,128)(2,1)}, u32[]{:S(2)}, u32[]{:S(2)}) collective-permute-start(bf16[2048,128]{1,0:T(8,128)(2,1)} %param.10), channel_id=1, source_target_pairs={{0,8},{8,16},{16,24},{24,32},{32,40},{40,48},{48,56},{56,64},{64,7... | collective-permute-start | bytes 1572872 | tf_op jit(solution)/shard_map/ppermute | solution.py:12
  14.7 78.9 %collective-permute-start = (bf16[2048,128]{1,0:T(8,128)(2,1)}, bf16[2048,128]{1,0:T(8,128)(2,1)S(1)}, u32[]{:S(2)}, u32[]{:S(2)}) collective-permute-start(bf16[2048,128]{1,0:T(8,128)(2,1)} %param.9), channel_id=1, source_target_pairs={{0,8},{8,16},{16,24},{24,32},{32,40},{40,48},{48,56},{56,64},{64,7... | collective-permute-start | bytes 1572872 | tf_op jit(solution)/shard_map/ppermute | solution.py:12
  48.5 15.4 %all-to-all-start = ((bf16[256,8,128]{0,2,1:T(8,128)(2,1)}), bf16[256,8,128]{0,2,1:T(8,128)(2,1)S(1)}, u32[]{:S(2)}, u32[]{:S(2)}) async-start(bf16[256,8,128]{0,2,1:T(8,128)(2,1)} %bitcast), calls=%async_computation | async-start | bytes 1048576 | tf_op jit(solution)/shard_map/all_to_all | solution.py:100
  54.2 115.8 %reduce-scatter.3.cloned.1.call-start = ((), (), s32[]{:S(2)}) async-start(), calls=%async_computation.5 | async-start | bytes 1179648 | tf_op jit(solution)/shard_map/reduce_scatter | solution.py:148
  73.1 6.3 %copy-start.22 = (bf16[4,256,128]{2,1,0:T(8,128)(2,1)S(1)}, bf16[4,256,128]{2,1,0:T(8,128)(2,1)}, u32[]{:S(2)}) copy-start(bf16[4,256,128]{2,1,0:T(8,128)(2,1)} %copy-done.21) | copy-start | bytes 786436
  93.5 3.9 %copy-start.9 = (bf16[2048,128]{1,0:T(8,128)(2,1)}, bf16[2048,128]{1,0:T(8,128)(2,1)S(1)}, u32[]{:S(2)}) copy-start(bf16[2048,128]{1,0:T(8,128)(2,1)S(1)} %collective-permute-done) | copy-start | bytes 1572868
  94.2 3.2 %copy-start.16 = (f32[1024,1024]{1,0:T(8,128)}, f32[1024,1024]{1,0:T(8,128)S(1)}, u32[]{:S(2)}) copy-start(f32[1024,1024]{1,0:T(8,128)S(1)} %fusion.175) | copy-start | bytes 12582916
  96.7 3.8 %copy-start = (bf16[1,1024,1024]{1,2,0:T(8,128)(2,1)}, bf16[1,1024,1024]{1,2,0:T(8,128)(2,1)S(1)}, u32[]{:S(2)}) copy-start(bf16[1,1024,1024]{1,2,0:T(8,128)(2,1)S(1)} %fusion.2) | copy-start | bytes 6291460
  98.2 3.1 %copy-start.10 = (bf16[2048,128]{1,0:T(8,128)(2,1)S(1)}, bf16[2048,128]{1,0:T(8,128)(2,1)}, u32[]{:S(2)}) copy-start(bf16[2048,128]{1,0:T(8,128)(2,1)} %copy-done.9) | copy-start | bytes 1572868
  104.2 3.7 %copy-start.2 = (bf16[1,1024,1024]{1,2,0:T(8,128)(2,1)}, bf16[1,1024,1024]{1,2,0:T(8,128)(2,1)S(1)}, u32[]{:S(2)}) copy-start(bf16[1,1024,1024]{1,2,0:T(8,128)(2,1)S(1)} %fusion.4) | copy-start | bytes 6291460
  108.7 12.6 %collective-permute-start.2 = (f32[2048,128]{1,0:T(8,128)S(1)}, f32[2048,128]{1,0:T(8,128)S(1)}, u32[]{:S(2)}, u32[]{:S(2)}) collective-permute-start(f32[2048,128]{1,0:T(8,128)S(1)} %pad_maximum_fusion), channel_id=1, source_target_pairs={{0,248},{8,0},{16,8},{24,16},{32,24},{40,32},{48,40},{56,48},{64,5... | collective-permute-start | bytes 3145736 | tf_op jit(solution)/shard_map/ppermute | solution.py:12
  122.5 5.6 %copy-start.12 = (f32[1024,128]{1,0:T(8,128)S(1)}, f32[1024,128]{1,0:T(8,128)}, u32[]{:S(2)}) copy-start(f32[1024,128]{1,0:T(8,128)} %fusion.64) | copy-start | bytes 1572868
  122.5 98.6 %reduce-scatter.5.cloned.1.call-start = ((), (), s32[]{:S(2)}) async-start(), calls=%async_computation.6 | async-start | bytes 1179648 | tf_op jit(solution)/shard_map/reduce_scatter | solution.py:149
  122.6 3.4 %copy-start.20 = (f32[1024,128]{1,0:T(8,128)S(1)}, f32[1024,128]{1,0:T(8,128)}, u32[]{:S(2)}) copy-start(f32[1024,128]{1,0:T(8,128)} %fusion.146) | copy-start | bytes 1572868
  122.6 5.5 %copy-start.7 = (bf16[1,1024,1024]{1,2,0:T(8,128)(2,1)S(1)}, bf16[1,1024,1024]{1,2,0:T(8,128)(2,1)}, u32[]{:S(2)}) copy-start(bf16[1,1024,1024]{1,2,0:T(8,128)(2,1)} %copy-done.6) | copy-start | bytes 6291460
  126.0 3.6 %copy-start.15 = (f32[1024,1024]{1,0:T(8,128)S(1)}, f32[1024,1024]{1,0:T(8,128)}, u32[]{:S(2)}) copy-start(f32[1024,1024]{1,0:T(8,128)} %fusion.184) | copy-start | bytes 12582916
  126.0 3.6 %copy-start.24 = (bf16[4,256,128]{2,1,0:T(8,128)(2,1)S(1)}, bf16[4,256,128]{2,1,0:T(8,128)(2,1)}, u32[]{:S(2)}) copy-start(bf16[4,256,128]{2,1,0:T(8,128)(2,1)} %copy.16) | copy-start | bytes 786436
  126.0 3.6 %copy-start.28 = (f32[1024,128]{1,0:T(8,128)S(1)}, f32[1024,128]{1,0:T(8,128)}, u32[]{:S(2)}) copy-start(f32[1024,128]{1,0:T(8,128)} %fusion.72) | copy-start | bytes 1572868
  126.1 14.3 %collective-permute-start.3 = (f32[2048,128]{1,0:T(8,128)S(1)}, f32[2048,128]{1,0:T(8,128)S(1)}, u32[]{:S(2)}, u32[]{:S(2)}) collective-permute-start(f32[2048,128]{1,0:T(8,128)S(1)} %pad_maximum_fusion.1), channel_id=1, source_target_pairs={{0,248},{8,0},{16,8},{24,16},{32,24},{40,32},{48,40},{56,48},{64,5... | collective-permute-start | bytes 3145736 | tf_op jit(solution)/shard_map/ppermute | solution.py:12
  132.8 8.6 %copy-start.11 = (bf16[2048,128]{1,0:T(8,128)(2,1)S(1)}, bf16[2048,128]{1,0:T(8,128)(2,1)}, u32[]{:S(2)}) copy-start(bf16[2048,128]{1,0:T(8,128)(2,1)} %copy-done.9) | copy-start | bytes 1572868
  141.5 2.3 %copy-start.1 = (bf16[1,1024,1024]{1,2,0:T(8,128)(2,1)S(1)}, bf16[1,1024,1024]{1,2,0:T(8,128)(2,1)}, u32[]{:S(2)}) copy-start(bf16[1,1024,1024]{1,2,0:T(8,128)(2,1)} %copy-done) | copy-start | bytes 6291460
  (14 other events, 26.4 us)
Sparse Core Ops, SparseCore 0:
  122.6 47.3 reduce-scatter.2
  172.6 48.5 reduce-scatter.4
where the time goes:
time: 233 us; the launch traced here: 230 us
  waiting for transfers between devices  82 us (35%)
  matrix products  54.4 us (23%)
  between operations  41.6 us (18%)
  starting transfers between devices  16 us (7%)
  blocking collectives  14.9 us (6%)
  local copies, waits for them, and re-layouts  13.9 us (6%)
  other arithmetic  6.94 us (3%)
    reduce_scatter x1, waiting for transfers between devices, body(): lax.psum_scatter(value_sum, 'uly', scatter_dimension=0, tiled=True)  49.6 us
    dot_general x8, matrix products, tile_gradients(): jnp.einsum('qhd,kd->hqk', g_tile, v_tile, preferred_element_type=jnp.floa...  15.8 us
    ppermute x4, waiting for transfers between devices, shifted(): return lax.ppermute(value, axis, pairs)  15.5 us
    all_to_all x1, blocking collectives, body(): lax.all_to_all(query_half_rows, 'uly', split_axis=0, concat_axis=1, tiled...  14.9 us
    dot_general x8, matrix products, tile_gradients(): jnp.einsum('hqk,qhd->kd', probs.astype(jnp.bfloat16), g_tile, preferred_e...  12.6 us
    dot_general x8, matrix products, tile_gradients(): jnp.einsum('qhd,kd->hqk', q_tile, k_tile, preferred_element_type=jnp.floa...  11.7 us
    all_to_all x1, waiting for transfers between devices, body(): lax.all_to_all(query_rows, 'uly', split_axis=1, concat_axis=0, tiled=True)  8.82 us
    unnamed x62, local copies, waits for them, and re-layouts  8.43 us
  transfers between devices with their start and end apart: 8, of which 5 were waited for; matrix products, arithmetic and copies ran while one was open for 23% of the time, Pallas kernels for 0%

commit v1 on v0

v1 whole, which is shorter than its diff:
```python
import functools
import math

import jax
import jax.numpy as jnp
from jax import lax
from jax.experimental import pallas as pl
from jax.experimental.pallas import tpu as pltpu
from jax.sharding import PartitionSpec as P

BF16 = jnp.bfloat16
F32 = jnp.float32
BIG = 2.0**100
HEADS = 8
DH = 128
ROWS = 256
PIECE = 128
PARTS = 2
COLS = HEADS * PIECE
GROUPS = 32
SCALE = 1.0 / math.sqrt(DH)
EXP_SCALE = SCALE * math.log2(math.e)


def dot(a, b):
    return jnp.dot(a, b, preferred_element_type=F32)


def three_terms(column):
    high = column.astype(BF16)
    rest = column - high.astype(F32)
    middle = rest.astype(BF16)
    low = (rest - middle.astype(F32)).astype(BF16)
    return high.astype(F32), middle.astype(F32), low.astype(F32)


def extra_columns(column, lane):
    high, middle, low = three_terms(column)
    block = jnp.where(lane == 0, high, jnp.where(lane == 1, middle, jnp.where(lane == 2, low, 0.0)))
    return jnp.where(lane == 3, 1.0, block).astype(BF16)


def kernel(
    order_ref, table_ref, q_ref, k_ref, v_ref, o_ref, g_ref, norm_ref,
    dq_ref, dk_ref, dv_ref,
    o_all, norm_all, k_nat, v_nat, k_aug, v_aug, q_aug, g_aug, q_t, g_t, mask_add,
    dq_acc, acc, stage1, stage2, chip_in, recv1, recv2, zsend, zrecv,
    o_send, o_recv, n_send, n_recv, kv_send, kv_recv, c_send, c_recv,
    r1_send, r1_recv, r1_local, r2_send, r2_recv, r2_local, z_send, z_recv,
):
    b = lax.axis_index("blk")
    u = lax.axis_index("uly")
    core = lax.rem(b, 2)
    even = core == 0
    even_b = b - core
    mate = b + 1 - 2 * core
    after = lax.rem(b + 1, GROUPS)
    before = lax.rem(b + GROUPS - 1, GROUPS)
    ux = u // 2
    uy = lax.rem(u, 2)
    peers = []
    for dx, dy in ((0, 1), (1, 0), (3, 0), (1, 1), (3, 1), (2, 0), (2, 1)):
        peers.append(lax.rem(ux + dx, 4) * 2 + lax.rem(uy + dy, 2))

    barrier = pltpu.get_barrier_semaphore()

    def greet(blk, uly):
        pl.semaphore_signal(barrier, inc=1, device_id={"blk": blk, "uly": uly})

    for peer in peers:
        greet(b, peer)
        greet(mate, peer)
    greet(after, u)
    greet(before, u)

    own_half = u // 4
    q_seq = order_ref[2 * b + own_half]

    def blocked(k_seq):
        seen = jnp.logical_and(k_seq < q_seq, table_ref[q_seq, k_seq] == 1)
        return jnp.where(seen, 0.0, -BIG)

    other_add = blocked(order_ref[2 * b + 1 - own_half])
    before_add0 = blocked(order_ref[2 * before])
    before_add1 = blocked(order_ref[2 * before + 1])

    sub = lax.broadcasted_iota(jnp.int32, (DH, COLS), 0)
    half_of = lax.broadcasted_iota(jnp.int32, (DH, COLS), 1) // (COLS // 2)

    def build_keys(slot, part, key_part, value_part, add0, add1):
        for owner in range(HEADS):
            cols = slice(owner * PIECE, (owner + 1) * PIECE)
            k_aug[slot, part, 0:DH, cols] = key_part(owner).T
            v_aug[slot, part, 0:DH, cols] = value_part(owner).T
        minus = jnp.where(sub < 3, -1.0, 0.0)
        add = jnp.where(half_of == 0, add0, add1)
        k_aug[slot, part, DH : 2 * DH, :] = jnp.where(sub == 3, add, minus).astype(BF16)
        v_aug[slot, part, DH : 2 * DH, :] = minus.astype(BF16)

    own_add0 = jnp.where(own_half == 0, 0.0, other_add)
    own_add1 = jnp.where(own_half == 0, other_add, 0.0)
    for part in range(PARTS):
        k_nat[core, part] = k_ref[:, part]
        v_nat[core, part] = v_ref[:, part]
        build_keys(
            core, part, lambda o: k_ref[o, part], lambda o: v_ref[o, part], own_add0, own_add1
        )
        row = lax.broadcasted_iota(jnp.int32, (ROWS, COLS), 0) + u * ROWS
        col = lax.broadcasted_iota(jnp.int32, (ROWS, COLS), 1)
        key = (col // PIECE) * ROWS + part * PIECE + col % PIECE
        hidden = jnp.logical_and(key // 1024 == own_half, key > row)
        mask_add[part] = jnp.where(hidden, -BIG, 0.0)
    q_t[...] = q_ref[...].T
    g_t[...] = g_ref[...].T
    dq_acc[...] = jnp.zeros_like(dq_acc)
    acc[...] = jnp.zeros_like(acc)
    o_all[u] = o_ref[u]
    norm_all[u] = norm_ref[u]

    pl.semaphore_wait(barrier, 16)

    kv_copies = []
    for part in range(PARTS):
        for which, (src, dst) in enumerate(((k_ref, k_nat), (v_ref, v_nat))):
            copy = pltpu.make_async_remote_copy(
                src_ref=src.at[:, part],
                dst_ref=dst.at[core, part],
                send_sem=kv_send.at[part, which],
                recv_sem=kv_recv.at[part, which],
                device_id={"blk": after, "uly": u},
            )
            copy.start()
            kv_copies.append(copy)
    o_copies = []
    for j, peer in enumerate(peers):
        for src, dst, send, recv in (
            (norm_ref, norm_all, n_send, n_recv),
            (o_ref, o_all, o_send, o_recv),
        ):
            copy = pltpu.make_async_remote_copy(
                src_ref=src.at[peer],
                dst_ref=dst.at[u],
                send_sem=send.at[j],
                recv_sem=recv.at[u],
                device_id={"blk": b, "uly": peer},
            )
            copy.start()
            o_copies.append(copy)

    def wait_into(dst, sem):
        pltpu.make_async_copy(dst, dst, sem).wait()

    def arrive_keys(part):
        slot = 1 - core
        for which, dst in enumerate((k_nat, v_nat)):
            wait_into(dst.at[slot, part], kv_recv.at[part, which])
        build_keys(
            slot, part, lambda o: k_nat[slot, part, o], lambda o: v_nat[slot, part, o],
            before_add0, before_add1,
        )

    lane = lax.broadcasted_iota(jnp.int32, (ROWS, DH), 1)

    def prepare(head):
        @pl.when(head != u)
        def _():
            wait_into(norm_all.at[head], n_recv.at[head])
            wait_into(o_all.at[head], o_recv.at[head])

        cols = pl.ds(pl.multiple_of(head * DH, DH), DH)
        q_head = q_ref[:, cols]
        g_head = g_ref[:, cols]
        norm = jnp.broadcast_to(norm_all[head], (DH, ROWS)).T / SCALE
        delta = jnp.sum(g_head.astype(F32) * o_all[head].astype(F32), axis=1, keepdims=True)
        q_aug[head, :, 0:DH] = q_head
        q_aug[head, :, DH : 2 * DH] = extra_columns(norm, lane)
        g_aug[head, :, 0:DH] = g_head
        g_aug[head, :, DH : 2 * DH] = extra_columns(delta, lane)

    def tile(slot, part, head, masked):
        rows = pl.ds(pl.multiple_of(head * DH, DH), DH)
        scores = dot(q_aug[head], k_aug[slot, part])
        if masked:
            scores = scores + mask_add[part]
        probs = jnp.exp2(scores * EXP_SCALE)
        grad_probs = dot(g_aug[head], v_aug[slot, part])
        grad_scores = (probs * grad_probs).astype(BF16)
        keys = k_nat[slot, part].reshape(COLS, DH)
        dq_acc[head] += dot(grad_scores, keys)
        return dot(q_t[rows], grad_scores), dot(g_t[rows], probs.astype(BF16))

    def pair_of(j):
        return lax.rem(ux + j + (j // 2) * (1 - 2 * lax.rem(j, 2)), 4)

    def pair_tiles(slot, part, pair, masked):
        key0, value0 = tile(slot, part, 2 * pair, masked)
        key1, value1 = tile(slot, part, 2 * pair + 1, masked)
        key_sum = key0 + key1
        value_sum = value0 + value1
        for owner in range(HEADS):
            cols = slice(owner * PIECE, (owner + 1) * PIECE)
            acc[slot, part, owner, 0:DH] += key_sum[:, cols]
            acc[slot, part, owner, DH : 2 * DH] += value_sum[:, cols]

    @pl.when(core == 1)
    def _():
        for part in range(PARTS):
            arrive_keys(part)

    def first_phase(masked):
        def step(j, carry):
            pair = pair_of(j)
            prepare(2 * pair)
            prepare(2 * pair + 1)
            for part in range(PARTS):
                pair_tiles(0, part, pair, masked)
            return carry

        lax.fori_loop(0, 4, step, 0)

    @pl.when(even)
    def _():
        first_phase(True)

    @pl.when(core == 1)
    def _():
        first_phase(False)

    mine = 4 * core
    theirs = 4 - mine
    for t in range(4):
        for part in range(PARTS):
            stage1[theirs + t, part] = acc[0, part, theirs + t].astype(BF16)
    chip_copy = pltpu.make_async_remote_copy(
        src_ref=stage1.at[pl.ds(theirs, 4)],
        dst_ref=chip_in,
        send_sem=c_send,
        recv_sem=c_recv,
        device_id={"blk": mate, "uly": u},
    )
    chip_copy.start()

    @pl.when(even)
    def _():
        arrive_keys(0)

    def second_phase(part, first, last, masked):
        def step(j, carry):
            pair_tiles(1, part, pair_of(j), masked)
            return carry

        lax.fori_loop(first, last, step, 0)

    def second(part, first, last):
        @pl.when(even)
        def _():
            second_phase(part, first, last, False)

        @pl.when(core == 1)
        def _():
            second_phase(part, first, last, True)

    second(0, 0, 1)

    chip_copy.wait()

    def r1_copy(t):
        owner = mine + t
        return pltpu.make_async_remote_copy(
            src_ref=stage1.at[owner],
            dst_ref=recv1.at[u],
            send_sem=r1_send.at[t],
            recv_sem=r1_recv.at[u],
            device_id={"blk": even_b, "uly": owner},
        )

    def is_self(t):
        return jnp.logical_and(even, mine + t == u)

    for t in range(4):
        owner = mine + t
        for part in range(PARTS):
            total = acc[0, part, owner] + chip_in[t, part].astype(F32)
            stage1[owner, part] = total.astype(BF16)

        @pl.when(jnp.logical_not(is_self(t)))
        def _():
            r1_copy(t).start()

    second(0, 1, 4)

    r2_copies = []

    def send_second(part):
        for owner in range(HEADS):
            stage2[part, owner] = acc[1, part, owner].astype(BF16)
        for j, peer in enumerate(peers):
            copy = pltpu.make_async_remote_copy(
                src_ref=stage2.at[part, peer],
                dst_ref=recv2.at[part, u],
                send_sem=r2_send.at[part, j],
                recv_sem=r2_recv.at[part, u],
                device_id={"blk": b, "uly": peer},
            )
            copy.start()
            r2_copies.append(copy)

    send_second(0)

    @pl.when(even)
    def _():
        arrive_keys(1)

    second(1, 0, 4)
    send_second(1)

    for head in range(HEADS):
        dq_ref[:, head * DH : (head + 1) * DH] = (dq_acc[head] * SCALE).astype(BF16)

    def write(part, total):
        rows = slice(part * PIECE, (part + 1) * PIECE)
        dk_ref[rows, :] = (total[0:DH] * SCALE).T.astype(BF16)
        dv_ref[rows, :] = total[DH : 2 * DH].T.astype(BF16)

    @pl.when(even)
    def _():
        totals = [jnp.zeros((2 * DH, PIECE), F32) for _ in range(PARTS)]
        for sender in range(HEADS):
            local = jnp.logical_and(u == sender, u < 4)

            @pl.when(jnp.logical_not(local))
            def _():
                wait_into(recv1.at[sender], r1_recv.at[sender])

            @pl.when(local)
            def _():
                recv1[sender] = stage1[sender]

            for part in range(PARTS):
                totals[part] = totals[part] + recv1[sender, part].astype(F32)
        for part in range(PARTS):
            write(part, totals[part])

    for part in range(PARTS):
        total = acc[1, part, u]
        for peer in peers:
            wait_into(recv2.at[part, peer], r2_recv.at[part, peer])
            total = total + recv2[part, peer].astype(F32)

        def z_copy():
            return pltpu.make_async_remote_copy(
                src_ref=zsend.at[part],
                dst_ref=zrecv.at[part],
                send_sem=z_send.at[part],
                recv_sem=z_recv.at[part],
                device_id={"blk": before, "uly": u},
            )

        @pl.when(even)
        def _():
            zsend[part] = total.astype(BF16)
            z_copy().start()

        @pl.when(core == 1)
        def _():
            wait_into(zrecv.at[part], z_recv.at[part])
            write(part, total + zrecv[part].astype(F32))

    for copy in kv_copies + o_copies + r2_copies:
        copy.wait_send()
    for t in range(4):
        @pl.when(jnp.logical_not(is_self(t)))
        def _():
            r1_copy(t).wait_send()

    @pl.when(even)
    def _():
        for part in range(PARTS):
            wait_into(zsend.at[part], z_send.at[part])


def body(query_rows, key_rows, value_rows, forward_output, grad_output, log_normalizer, block_order, block_table):
    vmem = pl.BlockSpec(memory_space=pltpu.VMEM)
    smem = pl.BlockSpec(memory_space=pltpu.SMEM)
    dma = pltpu.SemaphoreType.DMA
    scratch = [
        pltpu.VMEM((HEADS, ROWS, DH), BF16),
        pltpu.VMEM((HEADS, 1, ROWS), F32),
        pltpu.VMEM((2, PARTS, HEADS, PIECE, DH), BF16),
        pltpu.VMEM((2, PARTS, HEADS, PIECE, DH), BF16),
        pltpu.VMEM((2, PARTS, 2 * DH, COLS), BF16),
        pltpu.VMEM((2, PARTS, 2 * DH, COLS), BF16),
        pltpu.VMEM((HEADS, ROWS, 2 * DH), BF16),
        pltpu.VMEM((HEADS, ROWS, 2 * DH), BF16),
        pltpu.VMEM((HEADS * DH, ROWS), BF16),
        pltpu.VMEM((HEADS * DH, ROWS), BF16),
        pltpu.VMEM((PARTS, ROWS, COLS), F32),
        pltpu.VMEM((HEADS, ROWS, DH), F32),
        pltpu.VMEM((2, PARTS, HEADS, 2 * DH, PIECE), F32),
        pltpu.VMEM((HEADS, PARTS, 2 * DH, PIECE), BF16),
        pltpu.VMEM((PARTS, HEADS, 2 * DH, PIECE), BF16),
        pltpu.VMEM((4, PARTS, 2 * DH, PIECE), BF16),
        pltpu.VMEM((HEADS, PARTS, 2 * DH, PIECE), BF16),
        pltpu.VMEM((PARTS, HEADS, 2 * DH, PIECE), BF16),
        pltpu.VMEM((PARTS, 2 * DH, PIECE), BF16),
        pltpu.VMEM((PARTS, 2 * DH, PIECE), BF16),
        dma((7,)), dma((HEADS,)),
        dma((7,)), dma((HEADS,)),
        dma((PARTS, 2)), dma((PARTS, 2)),
        dma, dma,
        dma((4,)), dma((HEADS,)), dma,
        dma((PARTS, 7)), dma((PARTS, HEADS)), dma,
        dma((PARTS,)), dma((PARTS,)),
    ]
    return pl.pallas_call(
        kernel,
        out_shape=(
            jax.ShapeDtypeStruct((ROWS, HEADS * DH), BF16),
            jax.ShapeDtypeStruct((ROWS, DH), BF16),
            jax.ShapeDtypeStruct((ROWS, DH), BF16),
        ),
        in_specs=[smem, smem] + [vmem] * 6,
        out_specs=(vmem, vmem, vmem),
        scratch_shapes=scratch,
        compiler_params=pltpu.CompilerParams(
            collective_id=0, has_side_effects=True, vmem_limit_bytes=56 << 20
        ),
        cost_estimate=pl.CostEstimate(
            flops=10 * ROWS * HEADS * 4096 * DH,
            bytes_accessed=5 << 20,
            transcendentals=ROWS * HEADS * 4096,
        ),
    )(
        block_order,
        block_table,
        query_rows,
        key_rows.reshape(HEADS, PARTS, PIECE, DH),
        value_rows.reshape(HEADS, PARTS, PIECE, DH),
        forward_output.reshape(HEADS, ROWS, DH),
        grad_output,
        log_normalizer.reshape(HEADS, 1, ROWS),
    )


def solution(mesh):
    in_specs = (
        P(("blk", "uly"), None),
        P("blk", None),
        P("blk", None),
        P("blk", "uly"),
        P(("blk", "uly"), None),
        P("uly", "blk"),
        P(),
        P(),
    )
    out_specs = (P(("blk", "uly"), None), P(("blk", "uly"), None), P(("blk", "uly"), None))
    return jax.shard_map(body, mesh=mesh, in_specs=in_specs, out_specs=out_specs, check_vma=False)
```

time: 233 us -> 67.4 us (0.29)
  the two profiles are of different devices: /device:TPU:32 before, /device:TPU:1 now
where the time goes in v1:
time: 67.4 us; the launch traced here: 67.2 us
  Pallas kernels  63.1 us (94%)
  local copies, waits for them, and re-layouts  3.4 us (5%)
    pallas_call x1, Pallas kernels, body(): pl.pallas_call(kernel, out_shape=(jax.ShapeDtypeStruct((ROWS, HEADS * DH)...  63.1 us
    unnamed x7, local copies, waits for them, and re-layouts  3.4 us

profile of v1, /device:TPU:1, one launch (start us, length us, event | category | flops | bytes accessed | tf_op | source)
XLA Modules:
  0.0 67.2 jit_solution(6255981940464854533)
XLA Ops:
  0.6 63.1 %shard_map.103 = (bf16[256,1024]{1,0:T(8,128)(2,1)}, bf16[256,128]{1,0:T(8,128)(2,1)}, bf16[256,128]{1,0:T(8,128)(2,1)}) custom-call(s32[64]{0:T(128)} %order_ref.1, s32[64,64]{1,0:T(8,128)} %table_ref.1, bf16[256,1024]{1,0:T(8,128)(2,1)} %q_ref.1, bf16[8,2,128,128]{3,2,1,0:T(8,128)(2,1)} %bitcast.4, bf16[8,2,128,128]{3,2,1,0:T(8,128)(2,1)} %bitcast.5, ...), custom_call_target="tpu_custom_call" | custom-call | flops 10737418240 | bytes 5242880 | tf_op jit(solution)/shard_map/pallas_call | solution.py:415
  63.8 0.0 copy-start.1
  63.8 1.9 %copy.14 = bf16[256,1024]{1,0:T(8,128)(2,1)} copy(bf16[256,1024]{1,0:T(8,128)(2,1)} %get-tuple-element.6) | data formatting | bytes 1048576
  65.7 0.0 copy-done.1
  65.7 0.0 copy-start
  65.7 0.6 copy.15
  66.3 0.2 copy-done
  66.6 0.6 copy.16
Async XLA Ops:
  63.8 1.9 %copy-start.1 = (bf16[256,128]{1,0:T(8,128)(2,1)S(1)}, bf16[256,128]{1,0:T(8,128)(2,1)}, u32[]{:S(2)}) copy-start(bf16[256,128]{1,0:T(8,128)(2,1)} %get-tuple-element.7) | copy-start | bytes 196612
  65.7 0.9 %copy-start = (bf16[256,128]{1,0:T(8,128)(2,1)S(1)}, bf16[256,128]{1,0:T(8,128)(2,1)}, u32[]{:S(2)}) copy-start(bf16[256,128]{1,0:T(8,128)(2,1)} %get-tuple-element.8) | copy-start | bytes 196612

commit v2 on v1

v2 whole, which is shorter than its diff:
```python
import functools
import math

import jax
import jax.numpy as jnp
from jax import lax
from jax.experimental import pallas as pl
from jax.experimental.pallas import tpu as pltpu
from jax.sharding import PartitionSpec as P

BF16 = jnp.bfloat16
F32 = jnp.float32
BIG = 2.0**100
HEADS = 8
DH = 128
ROWS = 256
PIECE = 128
PARTS = 2
COLS = HEADS * PIECE
GROUPS = 32
PLANE = 16
SCALE = 1.0 / math.sqrt(DH)
EXP_SCALE = SCALE * math.log2(math.e)


def dot(a, b):
    return jnp.dot(a, b, preferred_element_type=F32)


def three_terms(column):
    high = column.astype(BF16)
    rest = column - high.astype(F32)
    middle = rest.astype(BF16)
    low = (rest - middle.astype(F32)).astype(BF16)
    return high.astype(F32), middle.astype(F32), low.astype(F32)


def extra_columns(column, lane):
    high, middle, low = three_terms(column)
    block = jnp.where(lane == 0, high, jnp.where(lane == 1, middle, jnp.where(lane == 2, low, 0.0)))
    return jnp.where(lane == 3, 1.0, block).astype(BF16)


def kernel(
    order_ref, table_ref, q_ref, k_ref, v_ref, o_ref, g_ref, norm_ref,
    dq_ref, dkv_ref,
    o_all, norm_all, kv_nat, k_aug, v_aug, q_aug, g_aug, q_t, g_t, mask_add,
    dq_acc, acc, probs_kept, stage1, stage2, chip_in, recv1, recv2, zsend, zrecv, sums,
    o_send, o_recv, n_send, n_recv, kv_send, kv_recv, w_send, w_recv, f_send, f_recv,
    c_send, c_recv, r1_send, r1_recv, r2_send, r2_recv, z_send, z_recv,
):
    b = lax.axis_index("blk")
    u = lax.axis_index("uly")
    core = lax.rem(b, 2)
    even = core == 0
    odd = core == 1
    even_b = b - core
    mate = b + 1 - 2 * core
    after = lax.rem(b + 1, GROUPS)
    before = lax.rem(b + GROUPS - 1, GROUPS)
    far_sender = lax.rem(b, PLANE) == PLANE - 1
    far_receiver = lax.rem(b, PLANE) == 0
    ux = u // 2
    uy = lax.rem(u, 2)
    peers = []
    for dx, dy in ((0, 1), (1, 0), (3, 0), (1, 1), (3, 1), (2, 0), (2, 1)):
        peers.append(lax.rem(ux + dx, 4) * 2 + lax.rem(uy + dy, 2))

    barrier = pltpu.get_barrier_semaphore()

    def greet(blk, uly):
        pl.semaphore_signal(barrier, inc=1, device_id={"blk": blk, "uly": uly})

    greet(mate, u)
    for peer in peers:
        greet(b, peer)
        greet(mate, peer)

    @pl.when(even)
    def _():
        greet(before, u)

    for part in range(PARTS):
        kv_nat[core, part, 0] = k_ref[:, part]
        kv_nat[core, part, 1] = v_ref[:, part]
    o_all[u] = o_ref[u]
    norm_all[u] = norm_ref[u]

    @pl.when(even)
    def _():
        pl.semaphore_wait(barrier, 15)

    @pl.when(odd)
    def _():
        pl.semaphore_wait(barrier, 16)

    def o_copies(j):
        peer = peers[j]
        copies = []
        for src, dst, send, recv in (
            (norm_ref, norm_all, n_send, n_recv),
            (o_ref, o_all, o_send, o_recv),
        ):
            copies.append(pltpu.make_async_remote_copy(
                src_ref=src.at[peer],
                dst_ref=dst.at[u],
                send_sem=send.at[j],
                recv_sem=recv.at[u],
                device_id={"blk": b, "uly": peer},
            ))
        return copies

    def kv_copy(part):
        return pltpu.make_async_remote_copy(
            src_ref=kv_nat.at[core, part],
            dst_ref=kv_nat.at[core, part],
            send_sem=kv_send.at[part],
            recv_sem=kv_recv.at[part],
            device_id={"blk": after, "uly": u},
        )

    def quarter(slot, half, x):
        return kv_nat.at[slot, half, :, pl.ds(2 * x, 2)]

    def far_copy(half):
        return pltpu.make_async_remote_copy(
            src_ref=quarter(core, half, ux),
            dst_ref=quarter(core, half, ux),
            send_sem=w_send.at[half],
            recv_sem=w_recv.at[half],
            device_id={"blk": after, "uly": u},
        )

    def forward_copy(half, dx):
        return pltpu.make_async_remote_copy(
            src_ref=quarter(1 - core, half, ux),
            dst_ref=quarter(1 - core, half, ux),
            send_sem=f_send.at[half, dx],
            recv_sem=f_recv.at[half, ux],
            device_id={"blk": b, "uly": lax.rem(ux + dx, 4) * 2 + uy},
        )

    @pl.when(far_sender)
    def _():
        for half in range(2):
            far_copy(half).start()

    @pl.when(jnp.logical_not(far_sender))
    def _():
        for part in range(PARTS):
            kv_copy(part).start()

    for j in range(7):
        for copy in o_copies(j):
            copy.start()

    own_half = u // 4
    q_seq = order_ref[2 * b + own_half]

    def blocked(k_seq):
        seen = jnp.logical_and(k_seq < q_seq, table_ref[q_seq, k_seq] == 1)
        return jnp.where(seen, 0.0, -BIG)

    other_add = blocked(order_ref[2 * b + 1 - own_half])
    before_add0 = blocked(order_ref[2 * before])
    before_add1 = blocked(order_ref[2 * before + 1])
    own_add0 = jnp.where(own_half == 0, 0.0, other_add)
    own_add1 = jnp.where(own_half == 0, other_add, 0.0)

    def build_keys(slot, part, add0, add1):
        sub = lax.broadcasted_iota(jnp.int32, (DH, COLS), 0)
        half_of = lax.broadcasted_iota(jnp.int32, (DH, COLS), 1) // (COLS // 2)
        k_aug[slot, part, 0:DH, :] = kv_nat[slot, part, 0].reshape(COLS, DH).T
        v_aug[slot, part, 0:DH, :] = kv_nat[slot, part, 1].reshape(COLS, DH).T
        minus = jnp.where(sub < 3, -1.0, 0.0)
        add = jnp.where(half_of == 0, add0, add1)
        k_aug[slot, part, DH : 2 * DH, :] = jnp.where(sub == 3, add, minus).astype(BF16)
        v_aug[slot, part, DH : 2 * DH, :] = minus.astype(BF16)

    def own_part(part, carry):
        build_keys(core, part, own_add0, own_add1)
        row = lax.broadcasted_iota(jnp.int32, (ROWS, COLS), 0) + u * ROWS
        col = lax.broadcasted_iota(jnp.int32, (ROWS, COLS), 1)
        key = (col // PIECE) * ROWS + part * PIECE + col % PIECE
        hidden = jnp.logical_and(col // (COLS // 2) == own_half, key > row)
        mask_add[part] = jnp.where(hidden, -BIG, 0.0)
        for which in range(2):
            acc[part, which] = jnp.zeros((DH, COLS), F32)
        return carry

    lax.fori_loop(0, PARTS, own_part, 0)
    for src, dst in ((q_ref, q_t), (g_ref, g_t)):
        turned = src[...].T
        for head in range(HEADS):
            cols = slice(head % 2 * ROWS, (head % 2 + 1) * ROWS)
            dst[head // 2, :, cols] = turned[head * DH : (head + 1) * DH]
    dq_acc[...] = jnp.zeros_like(dq_acc)

    def wait_into(dst, sem):
        pltpu.make_async_copy(dst, dst, sem).wait()

    def arrive_keys(half):
        slot = 1 - core

        @pl.when(far_receiver)
        def _():
            for dx in (1, 3, 2):
                x = lax.rem(ux + dx, 4)
                wait_into(quarter(slot, half, x), f_recv.at[half, x])

        @pl.when(jnp.logical_not(far_receiver))
        def _():
            wait_into(kv_nat.at[slot, half], kv_recv.at[half])

        build_keys(slot, half, before_add0, before_add1)

    lane = lax.broadcasted_iota(jnp.int32, (ROWS, DH), 1)

    def prepare(pair, member):
        head = 2 * pair + member

        @pl.when(head != u)
        def _():
            wait_into(norm_all.at[head], n_recv.at[head])
            wait_into(o_all.at[head], o_recv.at[head])

        cols = pl.ds(pl.multiple_of(head * DH, DH), DH)
        rows = slice(member * ROWS, (member + 1) * ROWS)
        q_head = q_ref[:, cols]
        g_head = g_ref[:, cols]
        norm = jnp.broadcast_to(norm_all[head], (DH, ROWS)).T / SCALE
        delta = jnp.sum(g_head.astype(F32) * o_all[head].astype(F32), axis=1, keepdims=True)
        q_aug[pair, rows, 0:DH] = q_head
        q_aug[pair, rows, DH : 2 * DH] = extra_columns(norm, lane)
        g_aug[pair, rows, 0:DH] = g_head
        g_aug[pair, rows, DH : 2 * DH] = extra_columns(delta, lane)

    def tile_probs(slot, part, pair, masked):
        scores = dot(q_aug[pair], k_aug[slot, part])
        if masked:
            scores = scores.reshape(2, ROWS, COLS) + mask_add[part][None]
            scores = scores.reshape(2 * ROWS, COLS)
        return jnp.exp2(scores * EXP_SCALE)

    def tile_keys(slot, part, pair, probs):
        grad_probs = dot(g_aug[pair], v_aug[slot, part])
        grad_scores = (probs * grad_probs).astype(BF16)
        dq_acc[pair] += dot(grad_scores, kv_nat[slot, part, 0].reshape(COLS, DH))
        return dot(q_t[pair], grad_scores)

    def tile_values(pair, probs):
        return dot(g_t[pair], probs.astype(BF16))

    def put_pieces(stage, total):
        for owner in range(HEADS):
            stage[owner] = total[:, owner * PIECE : (owner + 1) * PIECE].astype(BF16)

    def first_pairs(half, first, last, masked):
        def step(j, carry):
            pair = lax.rem(ux + j + (j // 2) * (1 - 2 * lax.rem(j, 2)), 4)
            if half == 0:
                prepare(pair, 0)
                prepare(pair, 1)
            probs = tile_probs(0, half, pair, masked)
            acc[half, 0] += tile_keys(0, half, pair, probs)
            acc[half, 1] += tile_values(pair, probs)
            return carry

        lax.fori_loop(first, last, step, 0)

    def first(half, first_pair, last_pair):
        @pl.when(even)
        def _():
            first_pairs(half, first_pair, last_pair, True)

        @pl.when(odd)
        def _():
            first_pairs(half, first_pair, last_pair, False)

    mine = 4 * core
    theirs = 4 - mine

    def chip_copy(half):
        return pltpu.make_async_remote_copy(
            src_ref=stage1.at[half, :, pl.ds(theirs, 4)],
            dst_ref=chip_in.at[half],
            send_sem=c_send.at[half],
            recv_sem=c_recv.at[half],
            device_id={"blk": mate, "uly": u},
        )

    def exchange(half):
        for which in range(2):
            put_pieces(stage1.at[half, which], acc[half, which])
        chip_copy(half).start()

    def r1_copy(half, t):
        owner = mine + t
        return pltpu.make_async_remote_copy(
            src_ref=stage1.at[half, :, owner],
            dst_ref=recv1.at[half, u],
            send_sem=r1_send.at[half, t],
            recv_sem=r1_recv.at[half, u],
            device_id={"blk": even_b, "uly": owner},
        )

    def is_self(t):
        return jnp.logical_and(even, mine + t == u)

    def combine(half):
        wait_into(chip_in.at[half], c_recv.at[half])
        for t in range(4):
            for which in range(2):
                total = stage1[half, which, mine + t].astype(F32) + chip_in[half, which, t].astype(F32)
                stage1[half, which, mine + t] = total.astype(BF16)

            @pl.when(jnp.logical_not(is_self(t)))
            def _():
                r1_copy(half, t).start()

    def r2_copy(part, which, j):
        peer = peers[j]
        return pltpu.make_async_remote_copy(
            src_ref=stage2.at[part, which, peer],
            dst_ref=recv2.at[part, which, u],
            send_sem=r2_send.at[part, which, j],
            recv_sem=r2_recv.at[part, which, u],
            device_id={"blk": b, "uly": peer},
        )

    def second_values(part, masked):
        total = None
        for pair in range(HEADS // 2):
            probs = tile_probs(1, part, pair, masked)
            probs_kept[pair] = probs
            term = tile_values(pair, probs)
            total = term if total is None else total + term
        put_pieces(stage2.at[part, 1], total)

    def second_keys(part):
        total = None
        for pair in range(HEADS // 2):
            term = tile_keys(1, part, pair, probs_kept[pair])
            total = term if total is None else total + term
        put_pieces(stage2.at[part, 0], total)

    @pl.when(odd)
    def _():
        arrive_keys(0)
        arrive_keys(1)

    first(0, 0, 4)
    exchange(0)
    first(1, 0, 1)
    combine(0)

    @pl.when(far_receiver)
    def _():
        for half in range(2):
            wait_into(quarter(1 - core, half, ux), w_recv.at[half])
            for dx in (1, 3, 2):
                forward_copy(half, dx).start()

    first(1, 1, 4)
    exchange(1)

    @pl.when(even)
    def _():
        arrive_keys(0)

    def second_step(part, carry):
        @pl.when(jnp.logical_and(even, part == 1))
        def _():
            arrive_keys(1)

        @pl.when(even)
        def _():
            second_values(part, False)

        @pl.when(odd)
        def _():
            second_values(part, True)

        @pl.when(part == 0)
        def _():
            combine(1)

        for j in range(7):
            r2_copy(part, 1, j).start()
        second_keys(part)
        for j in range(7):
            r2_copy(part, 0, j).start()
        return carry

    lax.fori_loop(0, PARTS, second_step, 0)

    for head in range(HEADS):
        rows = slice(head % 2 * ROWS, (head % 2 + 1) * ROWS)
        dq_ref[:, head * DH : (head + 1) * DH] = (dq_acc[head // 2, rows] * SCALE).astype(BF16)

    def write(part, which, total):
        rows = slice(part * PIECE, (part + 1) * PIECE)
        turned = total.T
        if which == 0:
            turned = turned * SCALE
        dkv_ref[which, rows, :] = turned.astype(BF16)

    @pl.when(even)
    def _():
        for half in range(2):
            for sender in range(HEADS):
                local = jnp.logical_and(u == sender, u < 4)

                @pl.when(jnp.logical_not(local))
                def _():
                    wait_into(recv1.at[half, sender], r1_recv.at[half, sender])

                @pl.when(local)
                def _():
                    for which in range(2):
                        recv1[half, sender, which] = stage1[half, which, sender]

            for which in range(2):
                total = recv1[half, 0, which].astype(F32)
                for sender in range(1, HEADS):
                    total = total + recv1[half, sender, which].astype(F32)
                write(half, which, total)

    def z_copy(part, which):
        return pltpu.make_async_remote_copy(
            src_ref=zsend.at[part, which],
            dst_ref=zrecv.at[part, which],
            send_sem=z_send.at[part, which],
            recv_sem=z_recv.at[part, which],
            device_id={"blk": before, "uly": u},
        )

    steps = [(part, which) for part in range(PARTS) for which in (1, 0)]
    for part, which in steps:
        total = stage2[part, which, u].astype(F32)
        for peer in peers:
            wait_into(recv2.at[part, which, peer], r2_recv.at[part, which, peer])
            total = total + recv2[part, which, peer].astype(F32)

        @pl.when(even)
        def _():
            zsend[part, which] = total.astype(BF16)
            z_copy(part, which).start()

        @pl.when(odd)
        def _():
            sums[part, which] = total

    @pl.when(odd)
    def _():
        for part, which in steps:
            wait_into(zrecv.at[part, which], z_recv.at[part, which])
            write(part, which, sums[part, which] + zrecv[part, which].astype(F32))

    for j in range(7):
        for copy in o_copies(j):
            copy.wait_send()

    @pl.when(far_sender)
    def _():
        for half in range(2):
            far_copy(half).wait_send()

    @pl.when(jnp.logical_not(far_sender))
    def _():
        for part in range(PARTS):
            kv_copy(part).wait_send()

    @pl.when(far_receiver)
    def _():
        for half in range(2):
            for dx in (1, 3, 2):
                forward_copy(half, dx).wait_send()

    for half in range(2):
        chip_copy(half).wait_send()
        for t in range(4):
            @pl.when(jnp.logical_not(is_self(t)))
            def _():
                r1_copy(half, t).wait_send()

    for part, which in steps:
        for j in range(7):
            r2_copy(part, which, j).wait_send()

        @pl.when(even)
        def _():
            z_copy(part, which).wait_send()


def hand_on(dq_in, dkv_in, dq_ref, dk_ref, dv_ref):
    dq_ref[...] = dq_in[...]
    dk_ref[...] = dkv_in[0]
    dv_ref[...] = dkv_in[1]


def body(query_rows, key_rows, value_rows, forward_output, grad_output, log_normalizer, block_order, block_table):
    vmem = pl.BlockSpec(memory_space=pltpu.VMEM)
    smem = pl.BlockSpec(memory_space=pltpu.SMEM)
    dma = pltpu.SemaphoreType.DMA
    piece = (DH, PIECE)
    scratch = [
        pltpu.VMEM((HEADS, ROWS, DH), BF16),
        pltpu.VMEM((HEADS, 1, ROWS), F32),
        pltpu.VMEM((2, PARTS, 2, HEADS, PIECE, DH), BF16),
        pltpu.VMEM((2, PARTS, 2 * DH, COLS), BF16),
        pltpu.VMEM((2, PARTS, 2 * DH, COLS), BF16),
        pltpu.VMEM((HEADS // 2, 2 * ROWS, 2 * DH), BF16),
        pltpu.VMEM((HEADS // 2, 2 * ROWS, 2 * DH), BF16),
        pltpu.VMEM((HEADS // 2, DH, 2 * ROWS), BF16),
        pltpu.VMEM((HEADS // 2, DH, 2 * ROWS), BF16),
        pltpu.VMEM((PARTS, ROWS, COLS), F32),
        pltpu.VMEM((HEADS // 2, 2 * ROWS, DH), F32),
        pltpu.VMEM((PARTS, 2, DH, COLS), F32),
        pltpu.VMEM((HEADS // 2, 2 * ROWS, COLS), F32),
        pltpu.VMEM((PARTS, 2, HEADS) + piece, BF16),
        pltpu.VMEM((PARTS, 2, HEADS) + piece, BF16),
        pltpu.VMEM((PARTS, 2, 4) + piece, BF16),
        pltpu.VMEM((PARTS, HEADS, 2) + piece, BF16),
        pltpu.VMEM((PARTS, 2, HEADS) + piece, BF16),
        pltpu.VMEM((PARTS, 2) + piece, BF16),
        pltpu.VMEM((PARTS, 2) + piece, BF16),
        pltpu.VMEM((PARTS, 2) + piece, F32),
        dma((7,)), dma((HEADS,)),
        dma((7,)), dma((HEADS,)),
        dma((PARTS,)), dma((PARTS,)),
        dma((2,)), dma((2,)),
        dma((2, 4)), dma((2, 4)),
        dma((2,)), dma((2,)),
        dma((2, 4)), dma((2, HEADS)),
        dma((PARTS, 2, 7)), dma((PARTS, 2, HEADS)),
        dma((PARTS, 2)), dma((PARTS, 2)),
    ]
    dq, dkv = pl.pallas_call(
        kernel,
        out_shape=(
            jax.ShapeDtypeStruct((ROWS, HEADS * DH), BF16),
            jax.ShapeDtypeStruct((2, ROWS, DH), BF16),
        ),
        in_specs=[smem, smem] + [vmem] * 6,
        out_specs=(vmem, vmem),
        scratch_shapes=scratch,
        compiler_params=pltpu.CompilerParams(
            collective_id=0, has_side_effects=True, vmem_limit_bytes=56 << 20
        ),
        cost_estimate=pl.CostEstimate(
            flops=10 * ROWS * HEADS * 4096 * DH,
            bytes_accessed=5 << 20,
            transcendentals=ROWS * HEADS * 4096,
        ),
    )(
        block_order,
        block_table,
        query_rows,
        key_rows.reshape(HEADS, PARTS, PIECE, DH),
        value_rows.reshape(HEADS, PARTS, PIECE, DH),
        forward_output.reshape(HEADS, ROWS, DH),
        grad_output,
        log_normalizer.reshape(HEADS, 1, ROWS),
    )
    rows_out = jax.ShapeDtypeStruct((ROWS, DH), BF16)
    return pl.pallas_call(
        hand_on,
        out_shape=(jax.ShapeDtypeStruct((ROWS, HEADS * DH), BF16), rows_out, rows_out),
        in_specs=[vmem, vmem],
        out_specs=(vmem, vmem, vmem),
    )(dq, dkv)


def solution(mesh):
    in_specs = (
        P(("blk", "uly"), None),
        P("blk", None),
        P("blk", None),
        P("blk", "uly"),
        P(("blk", "uly"), None),
        P("uly", "blk"),
        P(),
        P(),
    )
    out_specs = (P(("blk", "uly"), None), P(("blk", "uly"), None), P(("blk", "uly"), None))
    return jax.shard_map(body, mesh=mesh, in_specs=in_specs, out_specs=out_specs, check_vma=False)
```

time: 67.4 us -> 52.8 us (0.78)
  Pallas kernels: 63.1 us -> 51.5 us
  local copies, waits for them, and re-layouts: 3.4 us -> 0 us
    pallas_call x1, Pallas kernels: 63.1 us -> 49.6 us  [body(): pl.pallas_call(kernel, out_shape=(jax.ShapeDtypeStruct((ROWS, HEADS * DH)...]
    unnamed x7 -> x0, local copies, waits for them, and re-layouts: 3.4 us -> none
    pallas_call x0 -> x1, Pallas kernels: none -> 1.9 us  [body(): pl.pallas_call(hand_on, out_shape=(jax.ShapeDtypeStruct((ROWS, HEADS * DH...]
where the time goes in v2:
time: 52.8 us; the launch traced here: 52.1 us
  Pallas kernels  51.5 us (98%)
  between operations  0.64 us (1%)
    pallas_call x1, Pallas kernels, body(): pl.pallas_call(kernel, out_shape=(jax.ShapeDtypeStruct((ROWS, HEADS * DH)...  49.6 us
    pallas_call x1, Pallas kernels, body(): pl.pallas_call(hand_on, out_shape=(jax.ShapeDtypeStruct((ROWS, HEADS * DH...  1.9 us

profile of v2, /device:TPU:1, one launch (start us, length us, event | category | flops | bytes accessed | tf_op | source)
XLA Modules:
  0.0 52.1 jit_solution(8854696283685453507)
XLA Ops:
  0.6 49.6 %shard_map.103 = (bf16[256,1024]{1,0:T(8,128)(2,1)}, bf16[2,256,128]{2,1,0:T(8,128)(2,1)}) custom-call(s32[64]{0:T(128)} %order_ref.1, s32[64,64]{1,0:T(8,128)} %table_ref.1, bf16[256,1024]{1,0:T(8,128)(2,1)} %q_ref.1, bf16[8,2,128,128]{3,2,1,0:T(8,128)(2,1)} %bitcast.4, bf16[8,2,128,128]{3,2,1,0:T(8,128)(2,1)} %bitcast.5, bf16[8,256,128]{2,1,0:T(8,128)(2,1)} %bitcast.6, ...), custom_call_target="tpu_custom_call" | custom-call | flops 10737418240 | bytes 5242880 | tf_op jit(solution)/shard_map/pallas_call | solution.py:539
  50.2 1.9 %shard_map.104 = (bf16[256,1024]{1,0:T(8,128)(2,1)}, bf16[256,128]{1,0:T(8,128)(2,1)}, bf16[256,128]{1,0:T(8,128)(2,1)}) custom-call(bf16[256,1024]{1,0:T(8,128)(2,1)} %get-tuple-element.5.dq_in, bf16[2,256,128]{2,1,0:T(8,128)(2,1)} %get-tuple-element.6.dkv_in), custom_call_target="tpu_custom_call" | custom-call | tf_op jit(solution)/shard_map/pallas_call | solution.py:567

commit v3 on v2

--- a/solution.py
+++ b/solution.py
@@ -45,7 +45,7 @@
     order_ref, table_ref, q_ref, k_ref, v_ref, o_ref, g_ref, norm_ref,
     dq_ref, dkv_ref,
     o_all, norm_all, kv_nat, k_aug, v_aug, q_aug, g_aug, q_t, g_t, mask_add,
-    dq_acc, acc, probs_kept, stage1, stage2, chip_in, recv1, recv2, zsend, zrecv, sums,
+    dq_acc, acc, probs_kept, stage, chip_in, recv1, recv2, zsend, zrecv, sums,
     o_send, o_recv, n_send, n_recv, kv_send, kv_recv, w_send, w_recv, f_send, f_recv,
     c_send, c_recv, r1_send, r1_recv, r2_send, r2_recv, z_send, z_recv,
 ):
@@ -94,21 +94,23 @@
     def _():
         pl.semaphore_wait(barrier, 16)
 
-    def o_copies(j):
-        peer = peers[j]
-        copies = []
-        for src, dst, send, recv in (
-            (norm_ref, norm_all, n_send, n_recv),
-            (o_ref, o_all, o_send, o_recv),
-        ):
-            copies.append(pltpu.make_async_remote_copy(
-                src_ref=src.at[peer],
-                dst_ref=dst.at[u],
-                send_sem=send.at[j],
-                recv_sem=recv.at[u],
-                device_id={"blk": b, "uly": peer},
-            ))
-        return copies
+    def norm_copy(j):
+        return pltpu.make_async_remote_copy(
+            src_ref=norm_ref.at[peers[j]],
+            dst_ref=norm_all.at[u],
+            send_sem=n_send.at[j],
+            recv_sem=n_recv.at[u],
+            device_id={"blk": b, "uly": peers[j]},
+        )
+
+    def o_copy(j):
+        return pltpu.make_async_remote_copy(
+            src_ref=o_ref.at[peers[j]],
+            dst_ref=o_all.at[u],
+            send_sem=o_send.at[j],
+            recv_sem=o_recv.at[u],
+            device_id={"blk": b, "uly": peers[j]},
+        )
 
     def kv_copy(part):
         return pltpu.make_async_remote_copy(
@@ -140,6 +142,9 @@
             device_id={"blk": b, "uly": lax.rem(ux + dx, 4) * 2 + uy},
         )
 
+    for j in range(7):
+        norm_copy(j).start()
+
     @pl.when(far_sender)
     def _():
         for half in range(2):
@@ -151,8 +156,7 @@
             kv_copy(part).start()
 
     for j in range(7):
-        for copy in o_copies(j):
-            copy.start()
+        o_copy(j).start()
 
     own_half = u // 4
     q_seq = order_ref[2 * b + own_half]
@@ -184,8 +188,6 @@
         key = (col // PIECE) * ROWS + part * PIECE + col % PIECE
         hidden = jnp.logical_and(col // (COLS // 2) == own_half, key > row)
         mask_add[part] = jnp.where(hidden, -BIG, 0.0)
-        for which in range(2):
-            acc[part, which] = jnp.zeros((DH, COLS), F32)
         return carry
 
     lax.fori_loop(0, PARTS, own_part, 0)
@@ -216,22 +218,30 @@
 
     lane = lax.broadcasted_iota(jnp.int32, (ROWS, DH), 1)
 
-    def prepare(pair, member):
+    def prepare_queries(pair, member):
         head = 2 * pair + member
 
         @pl.when(head != u)
         def _():
             wait_into(norm_all.at[head], n_recv.at[head])
-            wait_into(o_all.at[head], o_recv.at[head])
 
         cols = pl.ds(pl.multiple_of(head * DH, DH), DH)
         rows = slice(member * ROWS, (member + 1) * ROWS)
-        q_head = q_ref[:, cols]
+        norm = jnp.broadcast_to(norm_all[head], (DH, ROWS)).T / SCALE
+        q_aug[pair, rows, 0:DH] = q_ref[:, cols]
+        q_aug[pair, rows, DH : 2 * DH] = extra_columns(norm, lane)
+
+    def prepare_grads(pair, member):
+        head = 2 * pair + member
+
+        @pl.when(head != u)
+        def _():
+            wait_into(o_all.at[head], o_recv.at[head])
+
+        cols = pl.ds(pl.multiple_of(head * DH, DH), DH)
+        rows = slice(member * ROWS, (member + 1) * ROWS)
         g_head = g_ref[:, cols]
-        norm = jnp.broadcast_to(norm_all[head], (DH, ROWS)).T / SCALE
         delta = jnp.sum(g_head.astype(F32) * o_all[head].astype(F32), axis=1, keepdims=True)
-        q_aug[pair, rows, 0:DH] = q_head
-        q_aug[pair, rows, DH : 2 * DH] = extra_columns(norm, lane)
         g_aug[pair, rows, 0:DH] = g_head
         g_aug[pair, rows, DH : 2 * DH] = extra_columns(delta, lane)
 
@@ -255,148 +265,155 @@
         for owner in range(HEADS):
             stage[owner] = total[:, owner * PIECE : (owner + 1) * PIECE].astype(BF16)
 
-    def first_pairs(half, first, last, masked):
-        def step(j, carry):
-            pair = lax.rem(ux + j + (j // 2) * (1 - 2 * lax.rem(j, 2)), 4)
-            if half == 0:
-                prepare(pair, 0)
-                prepare(pair, 1)
-            probs = tile_probs(0, half, pair, masked)
-            acc[half, 0] += tile_keys(0, half, pair, probs)
-            acc[half, 1] += tile_values(pair, probs)
+    def pair_of(j):
+        return lax.rem(ux + j + (j // 2) * (1 - 2 * lax.rem(j, 2)), 4)
+
+    def value_sums(step, slot, part, masked):
+        def two(i, carry):
+            pairs = (pair_of(2 * i), pair_of(2 * i + 1))
+
+            @pl.when(step == 0)
+            def _():
+                for pair in pairs:
+                    prepare_queries(pair, 0)
+                    prepare_queries(pair, 1)
+
+            total = None
+            for pair in pairs:
+                probs = tile_probs(slot, part, pair, masked)
+                probs_kept[pair] = probs
+                term = tile_values(pair, probs)
+                total = term if total is None else total + term
+            acc[1] += total
             return carry
 
-        lax.fori_loop(first, last, step, 0)
-
-    def first(half, first_pair, last_pair):
-        @pl.when(even)
-        def _():
-            first_pairs(half, first_pair, last_pair, True)
-
-        @pl.when(odd)
-        def _():
-            first_pairs(half, first_pair, last_pair, False)
+        lax.fori_loop(0, 2, two, 0)
+
+    def key_sums(step, slot, part):
+        def two(i, carry):
+            pairs = (pair_of(2 * i), pair_of(2 * i + 1))
+
+            @pl.when(step == 0)
+            def _():
+                for pair in pairs:
+                    prepare_grads(pair, 0)
+                    prepare_grads(pair, 1)
+
+            total = None
+            for pair in pairs:
+                term = tile_keys(slot, part, pair, probs_kept[pair])
+                total = term if total is None else total + term
+            acc[0] += total
+            return carry
+
+        lax.fori_loop(0, 2, two, 0)
 
     mine = 4 * core
     theirs = 4 - mine
 
-    def chip_copy(half):
-        return pltpu.make_async_remote_copy(
-            src_ref=stage1.at[half, :, pl.ds(theirs, 4)],
-            dst_ref=chip_in.at[half],
-            send_sem=c_send.at[half],
-            recv_sem=c_recv.at[half],
+    def chip_copy(half, which):
+        return pltpu.make_async_remote_copy(
+            src_ref=stage.at[0, half, which, pl.ds(theirs, 4)],
+            dst_ref=chip_in.at[half, which],
+            send_sem=c_send.at[half, which],
+            recv_sem=c_recv.at[half, which],
             device_id={"blk": mate, "uly": u},
         )
 
-    def exchange(half):
-        for which in range(2):
-            put_pieces(stage1.at[half, which], acc[half, which])
-        chip_copy(half).start()
-
-    def r1_copy(half, t):
+    def r1_copy(half, which, t):
         owner = mine + t
         return pltpu.make_async_remote_copy(
-            src_ref=stage1.at[half, :, owner],
-            dst_ref=recv1.at[half, u],
-            send_sem=r1_send.at[half, t],
-            recv_sem=r1_recv.at[half, u],
+            src_ref=stage.at[0, half, which, owner],
+            dst_ref=recv1.at[half, which, u],
+            send_sem=r1_send.at[half, which, t],
+            recv_sem=r1_recv.at[half, which, u],
             device_id={"blk": even_b, "uly": owner},
         )
 
     def is_self(t):
         return jnp.logical_and(even, mine + t == u)
 
-    def combine(half):
-        wait_into(chip_in.at[half], c_recv.at[half])
+    def combine(half, which):
+        wait_into(chip_in.at[half, which], c_recv.at[half, which])
         for t in range(4):
-            for which in range(2):
-                total = stage1[half, which, mine + t].astype(F32) + chip_in[half, which, t].astype(F32)
-                stage1[half, which, mine + t] = total.astype(BF16)
+            total = stage[0, half, which, mine + t].astype(F32) + chip_in[half, which, t].astype(F32)
+            stage[0, half, which, mine + t] = total.astype(BF16)
 
             @pl.when(jnp.logical_not(is_self(t)))
             def _():
-                r1_copy(half, t).start()
+                r1_copy(half, which, t).start()
 
     def r2_copy(part, which, j):
         peer = peers[j]
         return pltpu.make_async_remote_copy(
-            src_ref=stage2.at[part, which, peer],
+            src_ref=stage.at[1, part, which, peer],
             dst_ref=recv2.at[part, which, u],
             send_sem=r2_send.at[part, which, j],
             recv_sem=r2_recv.at[part, which, u],
             device_id={"blk": b, "uly": peer},
         )
 
-    def second_values(part, masked):
-        total = None
-        for pair in range(HEADS // 2):
-            probs = tile_probs(1, part, pair, masked)
-            probs_kept[pair] = probs
-            term = tile_values(pair, probs)
-            total = term if total is None else total + term
-        put_pieces(stage2.at[part, 1], total)
-
-    def second_keys(part):
-        total = None
-        for pair in range(HEADS // 2):
-            term = tile_keys(1, part, pair, probs_kept[pair])
-            total = term if total is None else total + term
-        put_pieces(stage2.at[part, 0], total)
-
-    @pl.when(odd)
-    def _():
-        arrive_keys(0)
-        arrive_keys(1)
-
-    first(0, 0, 4)
-    exchange(0)
-    first(1, 0, 1)
-    combine(0)
-
-    @pl.when(far_receiver)
-    def _():
-        for half in range(2):
-            wait_into(quarter(1 - core, half, ux), w_recv.at[half])
-            for dx in (1, 3, 2):
-                forward_copy(half, dx).start()
-
-    first(1, 1, 4)
-    exchange(1)
-
-    @pl.when(even)
-    def _():
-        arrive_keys(0)
-
-    def second_step(part, carry):
-        @pl.when(jnp.logical_and(even, part == 1))
-        def _():
-            arrive_keys(1)
-
-        @pl.when(even)
-        def _():
-            second_values(part, False)
-
-        @pl.when(odd)
-        def _():
-            second_values(part, True)
-
-        @pl.when(part == 0)
-        def _():
-            combine(1)
-
+    def send(part, which):
         for j in range(7):
-            r2_copy(part, 1, j).start()
-        second_keys(part)
-        for j in range(7):
-            r2_copy(part, 0, j).start()
+            r2_copy(part, which, j).start()
+
+    def run_step(step, carry):
+        middle = jnp.logical_or(step == 1, step == 2)
+        slot = jnp.where(even, step // 2, jnp.where(middle, 1, 0))
+        part = jnp.where(even, lax.rem(step, 2), step // 2)
+
+        for half in range(PARTS):
+            @pl.when(step == jnp.where(even, 2 + half, 3 * half))
+            def _():
+                arrive_keys(half)
+
+        acc[...] = jnp.zeros_like(acc)
+        own = slot == core
+
+        @pl.when(own)
+        def _():
+            value_sums(step, slot, part, True)
+
+        @pl.when(jnp.logical_not(own))
+        def _():
+            value_sums(step, slot, part, False)
+
+        def leave(which):
+            put_pieces(stage.at[slot, part, which], acc[which])
+
+            @pl.when(slot == 0)
+            def _():
+                chip_copy(part, which).start()
+
+            @pl.when(slot == 1)
+            def _():
+                send(part, which)
+
+        leave(1)
+
+        @pl.when(step == 1)
+        def _():
+            combine(0, 1)
+            combine(0, 0)
+
+            @pl.when(far_receiver)
+            def _():
+                for half in range(2):
+                    wait_into(quarter(1, half, ux), w_recv.at[half])
+                    for dx in (1, 3, 2):
+                        forward_copy(half, dx).start()
+
+        key_sums(step, slot, part)
+        leave(0)
         return carry
 
-    lax.fori_loop(0, PARTS, second_step, 0)
-
+    lax.fori_loop(0, 4, run_step, 0)
+    combine(1, 1)
     for head in range(HEADS):
         rows = slice(head % 2 * ROWS, (head % 2 + 1) * ROWS)
         dq_ref[:, head * DH : (head + 1) * DH] = (dq_acc[head // 2, rows] * SCALE).astype(BF16)
+
+    combine(1, 0)
 
     def write(part, which, total):
         rows = slice(part * PIECE, (part + 1) * PIECE)
@@ -405,26 +422,27 @@
             turned = turned * SCALE
         dkv_ref[which, rows, :] = turned.astype(BF16)
 
+    def finish_even(half, which):
+        for sender in range(HEADS):
+            local = jnp.logical_and(u == sender, u < 4)
+
+            @pl.when(jnp.logical_not(local))
+            def _():
+                wait_into(recv1.at[half, which, sender], r1_recv.at[half, which, sender])
+
+            @pl.when(local)
+            def _():
+                recv1[half, which, sender] = stage[0, half, which, sender]
+
+        total = recv1[half, which, 0].astype(F32)
+        for sender in range(1, HEADS):
+            total = total + recv1[half, which, sender].astype(F32)
+        write(half, which, total)
+
     @pl.when(even)
     def _():
-        for half in range(2):
-            for sender in range(HEADS):
-                local = jnp.logical_and(u == sender, u < 4)
-
-                @pl.when(jnp.logical_not(local))
-                def _():
-                    wait_into(recv1.at[half, sender], r1_recv.at[half, sender])
-
-                @pl.when(local)
-                def _():
-                    for which in range(2):
-                        recv1[half, sender, which] = stage1[half, which, sender]
-
-            for which in range(2):
-                total = recv1[half, 0, which].astype(F32)
-                for sender in range(1, HEADS):
-                    total = total + recv1[half, sender, which].astype(F32)
-                write(half, which, total)
+        finish_even(0, 1)
+        finish_even(0, 0)
 
     def z_copy(part, which):
         return pltpu.make_async_remote_copy(
@@ -437,7 +455,7 @@
 
     steps = [(part, which) for part in range(PARTS) for which in (1, 0)]
     for part, which in steps:
-        total = stage2[part, which, u].astype(F32)
+        total = stage[1, part, which, u].astype(F32)
         for peer in peers:
             wait_into(recv2.at[part, which, peer], r2_recv.at[part, which, peer])
             total = total + recv2[part, which, peer].astype(F32)
@@ -451,6 +469,11 @@
         def _():
             sums[part, which] = total
 
+    @pl.when(even)
+    def _():
+        finish_even(1, 1)
+        finish_even(1, 0)
+
     @pl.when(odd)
     def _():
         for part, which in steps:
@@ -458,8 +481,8 @@
             write(part, which, sums[part, which] + zrecv[part, which].astype(F32))
 
     for j in range(7):
-        for copy in o_copies(j):
-            copy.wait_send()
+        norm_copy(j).wait_send()
+        o_copy(j).wait_send()
 
     @pl.when(far_sender)
     def _():
@@ -477,12 +500,12 @@
             for dx in (1, 3, 2):
                 forward_copy(half, dx).wait_send()
 
-    for half in range(2):
-        chip_copy(half).wait_send()
+    for half, which in steps:
+        chip_copy(half, which).wait_send()
         for t in range(4):
             @pl.when(jnp.logical_not(is_self(t)))
             def _():
-                r1_copy(half, t).wait_send()
+                r1_copy(half, which, t).wait_send()
 
     for part, which in steps:
         for j in range(7):
@@ -516,12 +539,11 @@
         pltpu.VMEM((HEADS // 2, DH, 2 * ROWS), BF16),
         pltpu.VMEM((PARTS, ROWS, COLS), F32),
         pltpu.VMEM((HEADS // 2, 2 * ROWS, DH), F32),
-        pltpu.VMEM((PARTS, 2, DH, COLS), F32),
+        pltpu.VMEM((2, DH, COLS), F32),
         pltpu.VMEM((HEADS // 2, 2 * ROWS, COLS), F32),
+        pltpu.VMEM((2, PARTS, 2, HEADS) + piece, BF16),
+        pltpu.VMEM((PARTS, 2, 4) + piece, BF16),
         pltpu.VMEM((PARTS, 2, HEADS) + piece, BF16),
-        pltpu.VMEM((PARTS, 2, HEADS) + piece, BF16),
-        pltpu.VMEM((PARTS, 2, 4) + piece, BF16),
-        pltpu.VMEM((PARTS, HEADS, 2) + piece, BF16),
         pltpu.VMEM((PARTS, 2, HEADS) + piece, BF16),
         pltpu.VMEM((PARTS, 2) + piece, BF16),
         pltpu.VMEM((PARTS, 2) + piece, BF16),
@@ -531,8 +553,8 @@
         dma((PARTS,)), dma((PARTS,)),
         dma((2,)), dma((2,)),
         dma((2, 4)), dma((2, 4)),
-        dma((2,)), dma((2,)),
-        dma((2, 4)), dma((2, HEADS)),
+        dma((2, 2)), dma((2, 2)),
+        dma((2, 2, 4)), dma((2, 2, HEADS)),
         dma((PARTS, 2, 7)), dma((PARTS, 2, HEADS)),
         dma((PARTS, 2)), dma((PARTS, 2)),
     ]

time: 52.8 us -> 56.2 us (1.064)
  the two profiles are of different devices: /device:TPU:1 before, /device:TPU:8 now
where the time goes in v3:
time: 56.2 us; the launch traced here: 56.1 us
  Pallas kernels  55.4 us (99%)
  between operations  0.64 us (1%)
    pallas_call x1, Pallas kernels, body(): pl.pallas_call(kernel, out_shape=(jax.ShapeDtypeStruct((ROWS, HEADS * DH)...  53.5 us
    pallas_call x1, Pallas kernels, body(): pl.pallas_call(hand_on, out_shape=(jax.ShapeDtypeStruct((ROWS, HEADS * DH...  1.9 us

profile of v3, /device:TPU:8, one launch (start us, length us, event | category | flops | bytes accessed | tf_op | source)
XLA Modules:
  0.0 56.1 jit_solution(8862164461005679935)
XLA Ops:
  0.6 53.5 %shard_map.103 = (bf16[256,1024]{1,0:T(8,128)(2,1)}, bf16[2,256,128]{2,1,0:T(8,128)(2,1)}) custom-call(s32[64]{0:T(128)} %order_ref.1, s32[64,64]{1,0:T(8,128)} %table_ref.1, bf16[256,1024]{1,0:T(8,128)(2,1)} %q_ref.1, bf16[8,2,128,128]{3,2,1,0:T(8,128)(2,1)} %bitcast.4, bf16[8,2,128,128]{3,2,1,0:T(8,128)(2,1)} %bitcast.5, bf16[8,256,128]{2,1,0:T(8,128)(2,1)} %bitcast.6, ...), custom_call_target="tpu_custom_call" | custom-call | flops 10737418240 | bytes 5242880 | tf_op jit(solution)/shard_map/pallas_call | solution.py:561
  54.1 1.9 %shard_map.104 = (bf16[256,1024]{1,0:T(8,128)(2,1)}, bf16[256,128]{1,0:T(8,128)(2,1)}, bf16[256,128]{1,0:T(8,128)(2,1)}) custom-call(bf16[256,1024]{1,0:T(8,128)(2,1)} %get-tuple-element.5.dq_in, bf16[2,256,128]{2,1,0:T(8,128)(2,1)} %get-tuple-element.6.dkv_in), custom_call_target="tpu_custom_call" | custom-call | tf_op jit(solution)/shard_map/pallas_call | solution.py:589

commit v4 on v2

--- a/solution.py
+++ b/solution.py
@@ -385,10 +385,10 @@
         def _():
             combine(1)
 
-        for j in range(7):
+        for j in reversed(range(7)):
             r2_copy(part, 1, j).start()
         second_keys(part)
-        for j in range(7):
+        for j in reversed(range(7)):
             r2_copy(part, 0, j).start()
         return carry
 

time: 52.8 us -> 52.4 us (level)
  no operation moved by 1% of the time
where the time goes in v4:
time: 52.4 us; the launch traced here: 51.6 us
  Pallas kernels  51 us (97%)
  between operations  0.64 us (1%)
    pallas_call x1, Pallas kernels, body(): pl.pallas_call(kernel, out_shape=(jax.ShapeDtypeStruct((ROWS, HEADS * DH)...  49.1 us
    pallas_call x1, Pallas kernels, body(): pl.pallas_call(hand_on, out_shape=(jax.ShapeDtypeStruct((ROWS, HEADS * DH...  1.9 us

profile of v4, /device:TPU:1, one launch (start us, length us, event | category | flops | bytes accessed | tf_op | source)
XLA Modules:
  0.0 51.6 jit_solution(3936257522149810306)
XLA Ops:
  0.6 49.1 %shard_map.103 = (bf16[256,1024]{1,0:T(8,128)(2,1)}, bf16[2,256,128]{2,1,0:T(8,128)(2,1)}) custom-call(s32[64]{0:T(128)} %order_ref.1, s32[64,64]{1,0:T(8,128)} %table_ref.1, bf16[256,1024]{1,0:T(8,128)(2,1)} %q_ref.1, bf16[8,2,128,128]{3,2,1,0:T(8,128)(2,1)} %bitcast.4, bf16[8,2,128,128]{3,2,1,0:T(8,128)(2,1)} %bitcast.5, bf16[8,256,128]{2,1,0:T(8,128)(2,1)} %bitcast.6, ...), custom_call_target="tpu_custom_call" | custom-call | flops 10737418240 | bytes 5242880 | tf_op jit(solution)/shard_map/pallas_call | solution.py:539
  49.7 1.9 %shard_map.104 = (bf16[256,1024]{1,0:T(8,128)(2,1)}, bf16[256,128]{1,0:T(8,128)(2,1)}, bf16[256,128]{1,0:T(8,128)(2,1)}) custom-call(bf16[256,1024]{1,0:T(8,128)(2,1)} %get-tuple-element.5.dq_in, bf16[2,256,128]{2,1,0:T(8,128)(2,1)} %get-tuple-element.6.dkv_in), custom_call_target="tpu_custom_call" | custom-call | tf_op jit(solution)/shard_map/pallas_call | solution.py:567
